TPU v7x, 128 devices: a whole 4x4x4 slice. The times are simulated.
128 devices in a mesh: section: 2 (over y_hi), shard: 2 (over core), replica: 32 (over y_lo, z, x).
Axes of the slice: x: 4, y: 4 (y_hi: 2, y_lo: 2; y = y_hi * 2 + y_lo), z: 4, core: 2. Of those that a mesh axis runs over, the one named last changes fastest.
Arguments:
- inputs: bfloat16 [2, 64, 128, 1024], P(None, ('shard', 'replica')), may hold values from -6 to 6
- cotangent: bfloat16 [2, 64, 128, 1024], P(None, ('shard', 'replica')), may hold values from -6 to 6
- segments: int32 [2, 64, 128], P(None, ('shard', 'replica')), may hold values from 0 to 3, never falling along the last dimension, each value on 1 to 64 neighbouring positions
- routes: int32 [2, 2, 64, 128, 2], P('section', None, ('shard', 'replica')), may hold values from 0 to 2, all different within a row; in each aligned block of 128 rows (0 to 127, 128 to 255, ..., all dimensions but the last counted through in order) at most 96 rows name the same one
- mixer_gain: bfloat16 [2, 1024], P('section', 'shard'), may hold values from 0.5 to 1.5
- query_weight: bfloat16 [2, 1024, 1024], P('section', 'shard'), may hold values from -0.25 to 0.25
- key_matrix: bfloat16 [2, 1024, 512], P('section', 'shard'), may hold values from -0.25 to 0.25
- value_matrix: bfloat16 [2, 1024, 512], P('section', 'shard'), may hold values from -0.1875 to 0.1875
- out_weight: bfloat16 [2, 1024, 1024], P('section', 'shard'), may hold values from -0.375 to 0.375
- expert_gain: bfloat16 [2, 1024], P('section', 'shard'), may hold values from 0.5 to 1.5
- router_weight: bfloat16 [2, 1024, 3], P('section', 'shard'), may hold values from -0.125 to 0.125
- gate_weight: bfloat16 [2, 3, 1024, 512], P('section', None, 'shard'), may hold values from -0.1875 to 0.1875
- up_weight: bfloat16 [2, 3, 1024, 512], P('section', None, 'shard'), may hold values from -0.1875 to 0.1875
- down_weight: bfloat16 [2, 3, 512, 1024], P('section', None, 'shard'), may hold values from -0.5 to 0.5
Outputs:
- section_output: float32 [2, 2, 64, 128, 1024], P('section', None, ('shard', 'replica'))
- input_gradient: float32 [2, 2, 64, 128, 1024], P('section', None, ('shard', 'replica'))
- mixer_gain_gradient: float32 [2, 1024], P('section', 'shard')
- query_weight_gradient: float32 [2, 1024, 1024], P('section', 'shard')
- key_weight_gradient: float32 [2, 1024, 512], P('section', 'shard')
- value_weight_gradient: float32 [2, 1024, 512], P('section', 'shard')
- out_weight_gradient: float32 [2, 1024, 1024], P('section', 'shard')
- expert_gain_gradient: float32 [2, 1024], P('section', 'shard')
- router_weight_gradient: float32 [2, 1024, 3], P('section', 'shard')
- gate_weight_gradient: float32 [2, 3, 1024, 512], P('section', None, 'shard')
- up_weight_gradient: float32 [2, 3, 1024, 512], P('section', None, 'shard')
- down_weight_gradient: float32 [2, 3, 512, 1024], P('section', None, 'shard')
Inputs may be any that keep to these rules, and one draw needn't show every extreme that they name: `segments`: segment numbers never fall along a packed sequence; one segment spans half of 128 tokens. `routes`: each token names 2 different experts; within one packed sequence of one micro-batch and section, no expert is named by more than 96 tokens, a bound that some block reaches.
All inputs are finite; a program needn't handle non-finite values.
Results may differ from a plain program's by a relative error of at most 0.04.
Values may be sent and summed in bfloat16 or wider, within the bound.
A program may use at most 192 MiB of HBM per device.

v0:
```python
import functools

import numpy as np
import jax
import jax.numpy as jnp
from jax import lax
from jax.experimental import pallas as pl
from jax.experimental.pallas import tpu as pltpu
from jax.sharding import PartitionSpec as P

EPSILON = 1e-06
NT = (((1,), (1,)), ((), ()))
NN = (((1,), (0,)), ((), ()))
TN = (((0,), (0,)), ((), ()))
F32 = jnp.float32
BF16 = jnp.bfloat16
TOKENS = 256
WIDTH = 1024
VMEM_LIMIT = 62 * 1024 * 1024
MESH = pl.DeviceIdType.MESH
ROWS = 7680
COLS = 512
PARTS = 5
PART = ROWS // PARTS
DIMS = 5
KEY, VALUE, OUT, EXPERT, DOWN = 1024, 1536, 2048, 3072, 6144
PIECES = ((0, 1024), (1024, 1024), (2048, 1024), (3072, 1536), (4608, 1536), (6144, 1536))


def dot(a, b, dims):
    return lax.dot_general(a, b, dims, preferred_element_type=F32)


def scale_of(rows):
    return lax.rsqrt(jnp.mean(rows * rows, axis=-1, keepdims=True) + EPSILON)


def swap_halves(u):
    lanes = u.shape[1]
    lane = lax.broadcasted_iota(jnp.int32, u.shape, 1)
    return jnp.where(lane % 64 < 32, pltpu.roll(u, lanes - 32, 1), pltpu.roll(u, 32, 1))


def low_half(shape):
    return lax.broadcasted_iota(jnp.int32, shape, 1) < 64


def both_ways(block):
    wide = block.astype(F32)
    turned = pltpu.roll(wide, 64, 1)
    low = low_half(wide.shape)
    return jnp.where(low, wide, turned).astype(BF16), jnp.where(low, turned, wide).astype(BF16)


def stack_heads(block):
    wide = block.astype(F32)
    low = low_half(wide.shape)
    zero = jnp.zeros_like(wide)
    return jnp.concatenate([jnp.where(low, wide, zero), jnp.where(low, zero, wide)], axis=0).astype(BF16)


def join_heads(rows):
    return jnp.where(low_half((128, 128)), rows[:128], rows[128:])


def norm_back(rows, scale, gain, incoming):
    weighted = incoming * gain
    gain_part = jnp.sum(incoming * rows * scale, axis=0, keepdims=True)
    part = scale * weighted - rows * (scale * scale * scale) * jnp.mean(weighted * rows, axis=-1, keepdims=True)
    return part, gain_part


def cube_position():
    r = lax.axis_index("replica")
    x = r % 4
    z = (r // 4) % 4
    y = r // 16
    bits = (((x + 1) // 2) % 2, x // 2, ((z + 1) // 2) % 2, z // 2, y)
    partners = (
        r + 1 - 2 * (x % 2),
        r + 3 - 2 * x,
        r + 4 - 8 * (z % 2),
        r + 12 - 8 * z,
        (r + 16) % 32,
    )
    return bits, partners


def rows_at(at, count):
    if isinstance(at, int):
        return pl.ds(at, count)
    return pl.ds(pl.multiple_of(at, 16), count)


def add_rows(dst, dst_at, a, a_at, b, b_at, count):
    step = min(count, 192)

    def one(i, carry):
        at = i * step
        dst[rows_at(dst_at + at, step), :] = (
            a[rows_at(a_at + at, step), :] + b[rows_at(b_at + at, step), :]
        )
        return carry

    lax.fori_loop(0, count // step, one, 0)


def remote_copy(source, target, send_sem, recv_sem, device):
    return pltpu.make_async_remote_copy(
        src_ref=source, dst_ref=target, send_sem=send_sem, recv_sem=recv_sem,
        device_id=device, device_id_type=MESH,
    )


def layer_kernel(
    start_ref, loss_ref, segment_ref, route_ref, mixer_ref, expert_ref, router_ref, cos_ref, sin_ref,
    query_hbm, key_hbm, value_hbm, out_hbm, gate_hbm, up_hbm, down_hbm,
    output_hbm, gradient_hbm, total_hbm, small_out,
    pool, from_core, from_cube, whole, small_pair, small_mine, small_held, small_got,
    relayed, returned, relay, output, bias_ref,
    hidden_ref, normed_ref, q_ref, k_ref, v_ref, p_ref, att_ref, middle_ref, ne_ref, gl_ref, ul_ref, gi_ref,
    up_ref, bgu_ref, bb_ref, bqkv_ref, bne_ref, bm_ref, ba_ref, gradient,
    load_sem, weight_send, weight_recv, pair_send, pair_recv, relay_send, relay_recv,
    core_send, core_recv, cube_send, cube_recv, share_send, share_recv, small_send, small_recv, store_sem,
    output_sem,
):
    core = lax.axis_index("shard")
    section = lax.axis_index("section")
    bits, partners = cube_position()
    sibling = {"shard": 1 - core}
    other = {"section": 1 - section}

    barrier = pltpu.get_barrier_semaphore()
    pl.semaphore_signal(barrier, inc=1, device_id=sibling, device_id_type=MESH)
    pl.semaphore_signal(barrier, inc=1, device_id=other, device_id_type=MESH)
    for partner in partners:
        pl.semaphore_signal(barrier, inc=1, device_id={"replica": partner}, device_id_type=MESH)

    work = pool.at[core]
    loads = []

    def load(source, at, count):
        copy = pltpu.make_async_copy(source, work.at[pl.ds(at, count)], load_sem.at[len(loads)])
        copy.start()
        loads.append(copy)

    for i in range(2):
        load(query_hbm.at[:, pl.ds(i * 512, 512)], i * 512, 512)
    load(key_hbm, KEY, 512)
    load(value_hbm, VALUE, 512)
    for i in range(2):
        load(out_hbm.at[:, pl.ds(i * 512, 512)], OUT + i * 512, 512)
    for e in range(3):
        load(gate_hbm.at[e], EXPERT + e * 1024, 512)
        load(up_hbm.at[e], EXPERT + e * 1024 + 512, 512)
    for e in range(3):
        for i in range(2):
            load(down_hbm.at[e, :, pl.ds(i * 512, 512)], DOWN + e * 512 + i * 256, 256)
    needed = ((0, 1), (2, 3), (4, 5), (6, 7, 8), (9, 10, 11), (12, 13, 14, 15, 16, 17))

    pick = lax.broadcasted_iota(jnp.int32, (16, 3), 0) == lax.broadcasted_iota(jnp.int32, (16, 3), 1) + 2
    turned_router = dot(jnp.where(pick, 1.0, 0.0).astype(BF16), router_ref[...], NN)
    row = lax.broadcasted_iota(jnp.int32, (16, 512), 0)
    mixed = jnp.where(
        row == 0, mixer_ref[...].astype(F32), jnp.where(row == 1, expert_ref[...].astype(F32), turned_router)
    )
    small_pair[core] = mixed.astype(BF16)

    pl.semaphore_wait(barrier, 2 + DIMS)
    sends = []

    def remote(source, target, send_sem, recv_sem, device):
        copy = remote_copy(source, target, send_sem, recv_sem, device)
        copy.start()
        sends.append(copy)
        return copy

    pair = remote(small_pair.at[core], small_pair.at[core], pair_send, pair_recv, sibling)
    given = []

    def give():
        i = len(given)
        if i < len(PIECES):
            for index in needed[i]:
                loads[index].wait()
            rows = pl.ds(*PIECES[i])
            given.append(remote(work.at[rows], work.at[rows], weight_send.at[i], weight_recv.at[i], sibling))

    give()
    give()

    def arrive(i):
        given[i].wait_recv()
        give()

    position = lax.broadcasted_iota(jnp.int32, (128, 128), 0)
    earlier = lax.broadcasted_iota(jnp.int32, (128, 128), 1) <= position
    for pack in range(2):
        across = jnp.broadcast_to(segment_ref[pack:pack + 1, :].astype(F32), (128, 128))
        allowed = (across == jnp.transpose(across)) & earlier
        bias_ref[pack] = jnp.where(allowed, 0.0, -1e30)
    lane = lax.broadcasted_iota(jnp.int32, (TOKENS, 16), 1)
    expert_row = lax.broadcasted_iota(jnp.int32, (16, 128), 0)
    picked = []
    for pack in range(2):
        hit = (route_ref[pack, 0:1] + 2 == expert_row) | (route_ref[pack, 1:2] + 2 == expert_row)
        picked.append(jnp.transpose(jnp.where(hit, 1.0, 0.0)))
    marks = jnp.concatenate(picked, axis=0) > 0.0

    relays = [
        remote_copy(relay.at[i], relayed.at[i], relay_send.at[i], relay_recv.at[i], other) for i in range(2)
    ]
    returns = [
        remote_copy(relay.at[i], returned.at[i], relay_send.at[2 + i], relay_recv.at[2 + i], other)
        for i in range(2)
    ]

    @pl.when(section == 0)
    def _():
        hidden_ref[...] = start_ref[...]

    @pl.when(section == 1)
    def _():
        for i in range(2):
            relays[i].wait_recv()
            hidden_ref[:, i * 512:(i + 1) * 512] = relayed[i]

    pair.wait_recv()
    small = jnp.concatenate([small_pair[0], small_pair[1]], axis=1)
    x = hidden_ref[...].astype(F32)
    normed_ref[...] = (x * scale_of(x) * small[0:1].astype(F32)).astype(BF16)

    def through(a_ref, at, lanes):
        return dot(a_ref[:, 0:512], pool[0, at:at + 512, lanes], NN) + dot(
            a_ref[:, 512:1024], pool[1, at:at + 512, lanes], NN
        )

    quarters = (slice(0, 256), slice(256, 512))
    for j, (target, at, turned) in enumerate(
        ((q_ref, 0, True), (q_ref, 512, True), (k_ref, 0, True), (v_ref, 0, False))
    ):
        if j % 2 == 0:
            arrive(j // 2)
        for lanes in quarters:
            u = through(normed_ref, j * 512, lanes)
            if turned:
                u = u * cos_ref[...] + swap_halves(u) * sin_ref[...]
            target[:, at + lanes.start:at + lanes.stop] = u.astype(BF16)

    for pack in range(2):
        rows = slice(pack * 128, pack * 128 + 128)
        bias = jnp.concatenate([bias_ref[pack], bias_ref[pack]], axis=0)
        for pair_at in range(4):
            keys = both_ways(k_ref[rows, pair_at * 128:(pair_at + 1) * 128])
            values = both_ways(v_ref[rows, pair_at * 128:(pair_at + 1) * 128])
            for half in range(2):
                g = pair_at * 2 + half
                queries = stack_heads(q_ref[rows, g * 128:(g + 1) * 128])
                scores = dot(queries, keys[half], NT) * 0.125 + bias
                exponent = jnp.exp(scores - jnp.max(scores, axis=-1, keepdims=True))
                attention = (exponent / jnp.sum(exponent, axis=-1, keepdims=True)).astype(BF16)
                p_ref[pack, g] = attention
                att_ref[rows, g * 128:(g + 1) * 128] = join_heads(dot(attention, values[half], NN)).astype(BF16)

    arrive(2)
    for i in range(4):
        cols = slice(i * 256, (i + 1) * 256)
        middle_ref[:, cols] = hidden_ref[:, cols].astype(F32) + through(
            att_ref, OUT + (i // 2) * 512, quarters[i % 2]
        )
    middle = middle_ref[...]
    ne_ref[...] = (middle * scale_of(middle) * small[1:2].astype(F32)).astype(BF16)
    logits = dot(ne_ref[...], small, NT)
    peak = jnp.max(jnp.where(marks, logits, -1e30), axis=-1, keepdims=True)
    lifted = jnp.where(marks, jnp.exp(jnp.where(marks, logits - peak, 0.0)), 0.0)
    gates = lifted / jnp.sum(lifted, axis=-1, keepdims=True)

    for e in range(3):
        if e < 2:
            arrive(3 + e)
        for lanes in quarters:
            flat = slice(e * 512 + lanes.start, e * 512 + lanes.stop)
            gl = through(ne_ref, EXPERT + e * 1024, lanes)
            ul = through(ne_ref, EXPERT + e * 1024 + 512, lanes)
            gl_ref[:, flat] = gl.astype(BF16)
            ul_ref[:, flat] = ul.astype(BF16)
            inner = gl * jax.nn.sigmoid(gl) * ul
            gi_ref[:, flat] = (gates[:, 2 + e:3 + e] * inner).astype(BF16)

    arrive(5)
    for i in range(4):
        cols = slice(i * 256, (i + 1) * 256)
        total = middle_ref[:, cols]
        for e in range(3):
            at = DOWN + e * 512 + (i // 2) * 256
            for h in range(2):
                total = total + dot(
                    gi_ref[:, e * 512 + h * 256:e * 512 + (h + 1) * 256],
                    pool[h, at:at + 256, quarters[i % 2]], NN,
                )
        output[:, cols] = total
        relay[i // 2, :, quarters[i % 2]] = total.astype(BF16)
        if i % 2 == 1:
            @pl.when(section == 0)
            def _():
                relays[i // 2].start()

    output_copy = pltpu.make_async_copy(output, output_hbm, output_sem.at[0])
    output_copy.start()

    @pl.when(section == 0)
    def _():
        for i in range(2):
            relays[i].wait_send()
        for i in range(2):
            returns[i].wait_recv()
            up_ref[:, i * 512:(i + 1) * 512] = returned[i]

    @pl.when(section == 1)
    def _():
        up_ref[...] = loss_ref[...]

    pulls = jnp.zeros((TOKENS, 16), F32)
    for e in range(3):
        gate = gates[:, 2 + e:3 + e]
        for h in range(2):
            flat = slice(e * 512 + h * 256, e * 512 + (h + 1) * 256)
            at = DOWN + e * 512
            u = dot(up_ref[:, 0:512], pool[h, at:at + 256, :], NT) + dot(
                up_ref[:, 512:1024], pool[h, at + 256:at + 512, :], NT
            )
            gl = gl_ref[:, flat].astype(F32)
            ul = ul_ref[:, flat].astype(F32)
            sg = jax.nn.sigmoid(gl)
            silu = gl * sg
            pulls = pulls + jnp.where(lane == 2 + e, jnp.sum(u * silu * ul, axis=-1, keepdims=True), 0.0)
            inner = gate * u
            at = e * 1024 + h * 256
            bgu_ref[:, at:at + 256] = (inner * ul * sg * (1.0 + gl * (1.0 - sg))).astype(BF16)
            bgu_ref[:, at + 512:at + 768] = (inner * silu).astype(BF16)
    back_logits = (gates * (pulls - jnp.sum(gates * pulls, axis=-1, keepdims=True))).astype(BF16)

    for i in range(4):
        cols = slice(i * 256, (i + 1) * 256)
        h, inside = i // 2, (i % 2) * 256
        total = dot(back_logits, small[:, cols], NN)
        for j in range(6):
            at = EXPERT + j * 512 + inside
            total = total + dot(bgu_ref[:, j * 512:(j + 1) * 512], pool[h, at:at + 256, :], NT)
        bne_ref[:, cols] = total
    middle = middle_ref[...]
    part, expert_gain = norm_back(middle, scale_of(middle), small[1:2].astype(F32), bne_ref[...])
    bm_ref[...] = up_ref[...].astype(F32) + part
    bb_ref[...] = bm_ref[...].astype(BF16)

    for i in range(4):
        h, inside = i // 2, (i % 2) * 256
        total = dot(bb_ref[:, 0:512], pool[h, OUT + inside:OUT + inside + 256, :], NT)
        total = total + dot(bb_ref[:, 512:1024], pool[h, OUT + 512 + inside:OUT + inside + 768, :], NT)
        ba_ref[:, i * 256:(i + 1) * 256] = total.astype(BF16)

    cos, sin = cos_ref[0:128, 0:128], sin_ref[0:128, 0:128]

    def unturn(u):
        return (u * cos - swap_halves(u) * sin).astype(BF16)

    low = low_half((128, 128))
    for pack in range(2):
        rows = slice(pack * 128, pack * 128 + 128)
        for pair_at in range(4):
            keys = both_ways(k_ref[rows, pair_at * 128:(pair_at + 1) * 128])
            values = both_ways(v_ref[rows, pair_at * 128:(pair_at + 1) * 128])
            back_k, back_v = [], []
            for half in range(2):
                g = pair_at * 2 + half
                cols = slice(g * 128, (g + 1) * 128)
                queries = stack_heads(q_ref[rows, cols])
                back_out = stack_heads(ba_ref[rows, cols])
                attention = p_ref[pack, g]
                wide = attention.astype(F32)
                pull = dot(back_out, values[half], NT)
                bv = dot(attention, back_out, TN)
                back_v.append(bv + pltpu.roll(bv, 64, 1))
                spread = wide * pull
                back_scores = (
                    (spread - wide * jnp.sum(spread, axis=-1, keepdims=True)) * 0.125
                ).astype(BF16)
                bqkv_ref[rows, cols] = unturn(join_heads(dot(back_scores, keys[half], NN)))
                bk = dot(back_scores, queries, TN)
                back_k.append(bk + pltpu.roll(bk, 64, 1))
            at = 1024 + pair_at * 128
            bqkv_ref[rows, at:at + 128] = unturn(jnp.where(low, back_k[0], back_k[1]))
            bqkv_ref[rows, at + 512:at + 640] = jnp.where(low, back_v[0], back_v[1]).astype(BF16)

    for i in range(4):
        h, inside = i // 2, (i % 2) * 256
        total = jnp.zeros((TOKENS, 256), F32)
        for j in range(4):
            at = j * 512 + inside
            total = total + dot(bqkv_ref[:, j * 512:(j + 1) * 512], pool[h, at:at + 256, :], NT)
        bne_ref[:, i * 256:(i + 1) * 256] = total
    x = hidden_ref[...].astype(F32)
    part, mixer_gain = norm_back(x, scale_of(x), small[0:1].astype(F32), bne_ref[...])
    gradient[...] = bm_ref[...] + part
    for i in range(2):
        relay[i] = gradient[:, i * 512:(i + 1) * 512].astype(BF16)

    @pl.when(section == 1)
    def _():
        for i in range(2):
            returns[i].start()

    gradient_copy = pltpu.make_async_copy(gradient, gradient_hbm, output_sem.at[1])
    gradient_copy.start()
    router = dot(back_logits, ne_ref[...], TN)
    row = lax.broadcasted_iota(jnp.int32, router.shape, 0)
    mixed = jnp.where(row == 0, mixer_gain, jnp.where(row == 1, expert_gain, router))
    small_mine[0] = mixed[:, 0:512]
    small_mine[1] = mixed[:, 512:1024]

    def tiles(p, half):
        def tile(a, a_at, count, b, b_at, at):
            rows = a[:, pl.ds(pl.multiple_of(a_at, 256), count)]
            pool[half, at:at + count, :] = dot(rows, b[:, b_at:b_at + 512], TN).astype(BF16)

        left = half * 512
        if p == 0:
            for i in range(3):
                tile(normed_ref, left, 512, bqkv_ref, i * 512, i * 512)
        elif p == 1:
            tile(normed_ref, left, 512, bqkv_ref, 1536, VALUE)
            for i in range(2):
                tile(att_ref, left, 512, bb_ref, i * 512, OUT + i * 512)
        elif p < 4:
            for i in range(3 * p - 6, 3 * p - 3):
                tile(ne_ref, left, 512, bgu_ref, i * 512, EXPERT + i * 512)
        else:
            for e in range(3):
                for i in range(2):
                    tile(gi_ref, e * 512 + half * 256, 256, up_ref, i * 512, DOWN + e * 512 + i * 256)

    for copy in sends:
        copy.wait_send()
    sends.clear()
    lent = pool.at[1 - core]
    size = [PART >> s for s in range(DIMS + 1)]
    bit = [[bits[(p + s) % DIMS] for s in range(DIMS)] for p in range(PARTS)]
    device = [[{"replica": partners[(p + s) % DIMS]} for s in range(DIMS)] for p in range(PARTS)]
    held = [[p * PART] for p in range(PARTS)]
    for p in range(PARTS):
        for s in range(DIMS):
            held[p].append(held[p][s] + bit[p][s] * size[s + 1])

    def away(p, s):
        return held[p][s] + (1 - bit[p][s]) * size[s + 1]

    def core_piece(p, piece):
        at = away(p, 0) if piece == 0 else held[p][1]
        rows = rows_at(at, size[1])
        return remote(
            lent.at[rows], from_core.at[rows], core_send.at[2 * p + piece], core_recv.at[2 * p + piece], sibling
        )

    def slot(p, s, piece):
        return p * PART + PART - size[s] + piece * size[s + 2]

    def scatter(p, s):
        copies = []
        for piece in range(2 if s < DIMS - 1 else 1):
            index = (p * DIMS + s) * 2 + piece
            if s < DIMS - 1:
                b = bit[p][s + 1]
                at = away(p, s) + ((1 - b) if piece == 0 else b) * size[s + 2]
                count = size[s + 2]
                into = slot(p, s, piece)
            else:
                at, count, into = away(p, s), size[s + 1], p * PART + PART - size[s]
            copies.append(remote(
                work.at[rows_at(at, count)], from_cube.at[rows_at(into, count)],
                cube_send.at[index], cube_recv.at[index], device[p][s],
            ))
        return copies

    def share(p, s, at, piece):
        count = size[s + 2] if s < DIMS - 1 else size[DIMS]
        index = (p * DIMS + s) * 2 + piece
        rows = rows_at(at, count)
        return remote(whole.at[rows], whole.at[rows], share_send.at[index], share_recv.at[index], device[p][s])

    stores = []

    def store(at, count):
        rows = rows_at(at, count)
        copy = pltpu.make_async_copy(whole.at[rows], total_hbm.at[rows], store_sem.at[len(stores)])
        copy.start()
        stores.append(copy)

    small_copy = remote(small_mine.at[1 - core], small_got.at[0], small_send.at[0], small_recv.at[0], sibling)
    first = [None] * PARTS
    cube = [None] * PARTS

    def begin(p):
        first[p].wait_recv()
        at = away(p, 0)
        add_rows(work, at, work, at, from_core, at, size[1])
        cube[p] = scatter(p, 0)

    for p in range(PARTS):
        tiles(p, 1 - core)
        first[p] = core_piece(p, 0)
        tiles(p, core)
        if p > 0:
            begin(p - 1)
    second = [core_piece(p, 1) for p in range(PARTS)]
    begin(PARTS - 1)
    small_copy.wait_recv()
    small_held[0] = small_mine[core] + small_got[0]
    small_copy = remote(
        small_held.at[0], small_got.at[1], small_send.at[1], small_recv.at[1], {"replica": partners[0]}
    )
    for p in range(PARTS):
        second[p].wait_recv()
        at = held[p][1]
        add_rows(work, at, work, at, from_core, at, size[1])

    shared = [None] * PARTS
    for s in range(DIMS):
        later = [None] * PARTS
        for p in range(PARTS):
            copies = cube[p]
            copies[0].wait_recv()
            if s < DIMS - 1:
                at = away(p, s + 1)
                add_rows(work, at, work, at, from_cube, slot(p, s, 0), size[s + 2])
                later[p] = copies[1]
                cube[p] = scatter(p, s + 1)
            else:
                at = held[p][DIMS]
                add_rows(whole, at, work, at, from_cube, p * PART + PART - size[s], size[DIMS])
                shared[p] = {(s, 0): share(p, s, at, 0), (s - 1, 0): share(p, s - 1, at, 0)}
                store(at, size[DIMS])
        if s < DIMS - 1:
            for p in range(PARTS):
                later[p].wait_recv()
                at = held[p][s + 2]
                add_rows(work, at, work, at, from_cube, slot(p, s, 1), size[s + 2])
        small_copy.wait_recv()
        if s < DIMS - 1:
            small_held[s + 1] = small_held[s] + small_got[s + 1]
            small_copy = remote(
                small_held.at[s + 1], small_got.at[s + 2], small_send.at[s + 2], small_recv.at[s + 2],
                {"replica": partners[s + 1]},
            )
        else:
            small_out[...] = small_held[s] + small_got[s + 1]

    for s in reversed(range(DIMS)):
        for p in range(PARTS):
            shared[p][(s, 0)].wait_recv()
            if s < DIMS - 1:
                shared[p][(s, 1)].wait_recv()
            got = away(p, s)
            if s > 0:
                shared[p][(s - 1, 1)] = share(p, s - 1, got, 1)
            if s > 1:
                shared[p][(s - 2, 0)] = share(p, s - 2, held[p][s], 0)
            store(got, size[s + 1])

    @pl.when(section == 1)
    def _():
        for i in range(2):
            returns[i].wait_send()

    for copy in sends:
        copy.wait_send()
    for copy in stores:
        copy.wait()
    output_copy.wait()
    gradient_copy.wait()


def specs(places):
    return [pl.BlockSpec(memory_space=place) for place in places]


def both_layers(operands, weights):
    dma = pltpu.SemaphoreType.DMA
    wide, narrow = pltpu.VMEM((TOKENS, WIDTH), F32), pltpu.VMEM((TOKENS, WIDTH), BF16)
    halves = pltpu.VMEM((2, TOKENS, 512), BF16)
    buffer = pltpu.VMEM((ROWS, COLS), BF16)
    inner = pltpu.VMEM((TOKENS, 1536), BF16)
    return pl.pallas_call(
        layer_kernel,
        out_shape=(
            jax.ShapeDtypeStruct((TOKENS, WIDTH), F32),
            jax.ShapeDtypeStruct((TOKENS, WIDTH), F32),
            jax.ShapeDtypeStruct((ROWS, COLS), BF16),
            jax.ShapeDtypeStruct((16, COLS), F32),
        ),
        in_specs=specs([pltpu.VMEM] * len(operands) + [pl.ANY] * len(weights)),
        out_specs=tuple(specs([pl.ANY, pl.ANY, pl.ANY, pltpu.VMEM])),
        scratch_shapes=[
            pltpu.VMEM((2, ROWS, COLS), BF16), buffer, buffer, buffer,
            pltpu.VMEM((2, 16, COLS), BF16), pltpu.VMEM((2, 16, COLS), F32),
            pltpu.VMEM((DIMS, 16, COLS), F32), pltpu.VMEM((DIMS + 1, 16, COLS), F32),
            halves, halves, halves, wide, pltpu.VMEM((2, 128, 128), F32),
            narrow, narrow, narrow, pltpu.VMEM((TOKENS, 512), BF16), pltpu.VMEM((TOKENS, 512), BF16),
            pltpu.VMEM((2, 8, 256, 128), BF16), narrow, wide, narrow, inner, inner, inner,
            narrow, pltpu.VMEM((TOKENS, 3072), BF16), narrow, pltpu.VMEM((TOKENS, 2048), BF16),
            wide, wide, narrow, wide,
            dma((18,)), dma((6,)), dma((6,)), dma, dma, dma((4,)), dma((4,)),
            dma((2 * PARTS,)), dma((2 * PARTS,)),
            dma((2 * PARTS * DIMS,)), dma((2 * PARTS * DIMS,)),
            dma((2 * PARTS * DIMS,)), dma((2 * PARTS * DIMS,)),
            dma((DIMS + 1,)), dma((DIMS + 1,)),
            dma((PARTS + PARTS * DIMS,)), dma((2,)),
        ],
        compiler_params=pltpu.CompilerParams(
            collective_id=1, has_side_effects=True, vmem_limit_bytes=VMEM_LIMIT
        ),
    )(*operands, *weights)


def unpack_kernel(
    total_ref, small_ref, output_ref, gradient_ref, mixer_ref, query_ref, key_ref, value_ref, out_ref,
    expert_ref, router_ref, gate_ref, up_ref, down_ref, output_out, gradient_out,
    got, wide, passed, load_sem, store_sem,
):
    loads = []
    for i in range(15):
        rows = pl.ds(i * 512, 512)
        copy = pltpu.make_async_copy(total_ref.at[rows], got.at[rows], load_sem.at[i])
        copy.start()
        loads.append(copy)
    passes = [
        pltpu.make_async_copy(source, passed.at[i], load_sem.at[15 + i])
        for i, source in enumerate((output_ref, gradient_ref))
    ]
    for copy in passes:
        copy.start()
    stores = []

    def send(source, target):
        copy = pltpu.make_async_copy(source, target, store_sem.at[len(stores)])
        copy.start()
        stores.append(copy)

    small = small_ref[...]
    mixer_ref[...] = small[0:1]
    expert_ref[...] = small[1:2]
    for i in range(3):
        router_ref[i] = small[2 + i:3 + i]

    def put(at, count, target):
        wide[at:at + count, :] = got[at:at + count, :].astype(F32)
        send(wide.at[pl.ds(at, count)], target)

    for i in range(15):
        loads[i].wait()
        at = i * 512
        cols = pl.ds((i % 2) * 512, 512)
        if i < 2:
            put(at, 512, query_ref.at[:, cols])
        elif i == 2:
            put(at, 512, key_ref)
        elif i == 3:
            put(at, 512, value_ref)
        elif i < 6:
            put(at, 512, out_ref.at[:, cols])
        elif i < 12:
            e, which = (i - 6) // 2, (i - 6) % 2
            put(at, 512, (up_ref if which else gate_ref).at[e])
        else:
            for j in range(2):
                put(at + j * 256, 256, down_ref.at[i - 12, :, pl.ds(j * 512, 512)])
    for i, target in enumerate((output_out, gradient_out)):
        passes[i].wait()
        send(passed.at[i], target)
    for copy in stores:
        copy.wait()


def unpack(total, small, output, gradient):
    shapes = (
        (1, 512), (512, 1024), (512, 512), (512, 512), (512, 1024), (1, 512), (3, 1, 512),
        (3, 512, 512), (3, 512, 512), (3, 256, 1024), (TOKENS, WIDTH), (TOKENS, WIDTH),
    )
    places = [pl.ANY if i not in (0, 5, 6) else pltpu.VMEM for i in range(12)]
    return pl.pallas_call(
        unpack_kernel,
        out_shape=tuple(jax.ShapeDtypeStruct(shape, F32) for shape in shapes),
        in_specs=specs([pl.ANY, pltpu.VMEM, pl.ANY, pl.ANY]),
        out_specs=tuple(specs(places)),
        scratch_shapes=[
            pltpu.VMEM((ROWS, COLS), BF16), pltpu.VMEM((ROWS, COLS), F32), pltpu.VMEM((2, TOKENS, WIDTH), F32),
            pltpu.SemaphoreType.DMA((17,)), pltpu.SemaphoreType.DMA((20,)),
        ],
        compiler_params=pltpu.CompilerParams(vmem_limit_bytes=VMEM_LIMIT),
    )(total, small, output, gradient)


def rotary_tables():
    lane = np.arange(256)
    frequency = np.power(10000.0, -2.0 * (lane % 32) / 64.0)
    angles = (np.arange(TOKENS) % 128)[:, None] * frequency[None, :]
    sign = np.where(lane % 64 < 32, -1.0, 1.0)[None, :]
    return np.cos(angles).astype(np.float32), (np.sin(angles) * sign).astype(np.float32)


def body(
    inputs, cotangent, segments, routes, mixer_gain, query_weight, key_matrix, value_matrix, out_weight,
    expert_gain, router_weight, gate_weight, up_weight, down_weight,
):
    cos, sin = (jnp.asarray(table) for table in rotary_tables())
    operands = (
        inputs.reshape(TOKENS, WIDTH), cotangent.reshape(TOKENS, WIDTH), segments.reshape(2, 128),
        jnp.swapaxes(routes[0, :, 0], 1, 2), mixer_gain, expert_gain, jnp.transpose(router_weight[0]), cos, sin,
    )
    weights = (
        query_weight[0], key_matrix[0], value_matrix[0], out_weight[0], gate_weight[0], up_weight[0],
        down_weight[0],
    )
    output, gradient, total, small = both_layers(operands, weights)
    *owned, output, gradient = unpack(total, small, output, gradient)
    return (
        output.reshape(1, 2, 1, 128, WIDTH),
        gradient.reshape(1, 2, 1, 128, WIDTH),
        owned[0],
    ) + tuple(item[None] for item in owned[1:5]) + (owned[5],) + (
        jnp.transpose(owned[6][:, 0])[None],
    ) + tuple(item[None] for item in owned[7:])


def solution(mesh):
    return jax.shard_map(
        body,
        mesh=mesh,
        in_specs=(
            P(None, ("shard", "replica"), None, None),
            P(None, ("shard", "replica"), None, None),
            P(None, ("shard", "replica"), None),
            P("section", None, ("shard", "replica"), None, None),
            P("section", "shard"),
            P("section", "shard", None),
            P("section", "shard", None),
            P("section", "shard", None),
            P("section", "shard", None),
            P("section", "shard"),
            P("section", "shard", None),
            P("section", None, "shard", None),
            P("section", None, "shard", None),
            P("section", None, "shard", None),
        ),
        out_specs=(
            P("section", None, ("shard", "replica"), None, None),
            P("section", None, ("shard", "replica"), None, None),
            P("section", "shard"),
            P("section", "shard", None),
            P("section", "shard", None),
            P("section", "shard", None),
            P("section", "shard", None),
            P("section", "shard"),
            P("section", "shard", None),
            P("section", None, "shard", None),
            P("section", None, "shard", None),
            P("section", None, "shard", None),
        ),
        check_vma=False,
    )
```

profile of v0, /device:TPU:0, one launch (start us, length us, event | category | flops | bytes accessed | tf_op | source)
XLA Modules:
  0.0 178.7 jit_solution(14004567571585960478)
XLA Ops:
  0.6 165.9 %shard_map.247 = (f32[256,1024]{1,0:T(8,128)}, f32[256,1024]{1,0:T(8,128)}, bf16[7680,512]{1,0:T(8,128)(2,1)}, f32[16,512]{1,0:T(8,128)}) custom-call(bf16[256,1024]{1,0:T(8,128)(2,1)} %bitcast.41, bf16[256,1024]{1,0:T(8,128)(2,1)} %bitcast.42, s32[2,128]{1,0:T(2,128)} %bitcast.48, s32[2,2,128]{2,1,0:T(2,128)} %bitcast.47, bf16[1,512]{1,0:T(2,128)(2,1)} %mixer_ref.1, ...), custom_call_target="tpu_custom_call" | custom-call | tf_op jit(solution)/shard_map/pallas_call | solution.py:592
  166.6 10.8 %shard_map.248 = (f32[1,512]{1,0:T(1,128)}, f32[512,1024]{1,0:T(8,128)}, f32[512,512]{1,0:T(8,128)}, f32[512,512]{1,0:T(8,128)}, f32[512,1024]{1,0:T(8,128)}, /*...) custom-call(bf16[7680,512]{1,0:T(8,128)(2,1)} %get-tuple-element.28., ...), custom_call_target="tpu_custom_call" | custom-call | tf_op jit(solution)/shard_map/pallas_call | solution.py:689
  177.4 0.7 copy.33
  178.1 0.6 copy.30
where the time goes:
time: 179 us
  Pallas kernels  177 us (99%)
    pallas_call x1, Pallas kernels, both_layers(): pl.pallas_call(layer_kernel, out_shape=(jax.ShapeDtypeStruct((TOKENS, WID...  166 us
    pallas_call x1, Pallas kernels, unpack(): pl.pallas_call(unpack_kernel, out_shape=tuple((jax.ShapeDtypeStruct(shape...  10.8 us

commit v1 on v0

--- a/solution.py
+++ b/solution.py
@@ -117,7 +117,7 @@
     query_hbm, key_hbm, value_hbm, out_hbm, gate_hbm, up_hbm, down_hbm,
     output_hbm, gradient_hbm, total_hbm, small_out,
     pool, from_core, from_cube, whole, small_pair, small_mine, small_held, small_got,
-    relayed, returned, relay, output, bias_ref,
+    relayed, returned, relay, output, bias_ref, mark_ref, gate_ref,
     hidden_ref, normed_ref, q_ref, k_ref, v_ref, p_ref, att_ref, middle_ref, ne_ref, gl_ref, ul_ref, gi_ref,
     up_ref, bgu_ref, bb_ref, bqkv_ref, bne_ref, bm_ref, ba_ref, gradient,
     load_sem, weight_send, weight_recv, pair_send, pair_recv, relay_send, relay_recv,
@@ -177,21 +177,24 @@
 
     pair = remote(small_pair.at[core], small_pair.at[core], pair_send, pair_recv, sibling)
     given = []
-
-    def give():
-        i = len(given)
+    for i, (at, count) in enumerate(PIECES):
+        rows = pl.ds(at, count)
+        given.append(
+            remote_copy(work.at[rows], work.at[rows], weight_send.at[i], weight_recv.at[i], sibling)
+        )
+
+    def give(i):
         if i < len(PIECES):
             for index in needed[i]:
                 loads[index].wait()
-            rows = pl.ds(*PIECES[i])
-            given.append(remote(work.at[rows], work.at[rows], weight_send.at[i], weight_recv.at[i], sibling))
-
-    give()
-    give()
+            given[i].start()
 
     def arrive(i):
         given[i].wait_recv()
-        give()
+        give(i + 2)
+
+    give(0)
+    give(1)
 
     position = lax.broadcasted_iota(jnp.int32, (128, 128), 0)
     earlier = lax.broadcasted_iota(jnp.int32, (128, 128), 1) <= position
@@ -215,206 +218,222 @@
         for i in range(2)
     ]
 
+    pair.wait_recv()
+    small = jnp.concatenate([small_pair[0], small_pair[1]], axis=1)
+    mark_ref[...] = jnp.where(marks, 1.0, 0.0)
+
+    def through(a_ref, part, at, lanes):
+        return dot(a_ref[part, 0:512], pool[0, at:at + 512, lanes], NN) + dot(
+            a_ref[part, 512:1024], pool[1, at:at + 512, lanes], NN
+        )
+
+    quarters = (slice(0, 256), slice(256, 512))
+
+    def forward(part, ready):
+        x = hidden_ref[part, :].astype(F32)
+        normed_ref[part, :] = (x * scale_of(x) * small[0:1].astype(F32)).astype(BF16)
+
+        for j, (target, at, turned) in enumerate(
+            ((q_ref, 0, True), (q_ref, 512, True), (k_ref, 0, True), (v_ref, 0, False))
+        ):
+            if j % 2 == 0:
+                ready(j // 2)
+            for lanes in quarters:
+                u = through(normed_ref, part, j * 512, lanes)
+                if turned:
+                    u = u * cos_ref[part, :] + swap_halves(u) * sin_ref[part, :]
+                target[part, at + lanes.start:at + lanes.stop] = u.astype(BF16)
+
+        for pack in range(part.start // 128, part.stop // 128):
+            rows = slice(pack * 128, pack * 128 + 128)
+            bias = jnp.concatenate([bias_ref[pack], bias_ref[pack]], axis=0)
+            for pair_at in range(4):
+                keys = both_ways(k_ref[rows, pair_at * 128:(pair_at + 1) * 128])
+                values = both_ways(v_ref[rows, pair_at * 128:(pair_at + 1) * 128])
+                for half in range(2):
+                    g = pair_at * 2 + half
+                    queries = stack_heads(q_ref[rows, g * 128:(g + 1) * 128])
+                    scores = dot(queries, keys[half], NT) * 0.125 + bias
+                    exponent = jnp.exp(scores - jnp.max(scores, axis=-1, keepdims=True))
+                    attention = (exponent / jnp.sum(exponent, axis=-1, keepdims=True)).astype(BF16)
+                    p_ref[pack, g] = attention
+                    att_ref[rows, g * 128:(g + 1) * 128] = join_heads(dot(attention, values[half], NN)).astype(BF16)
+
+        ready(2)
+        for i in range(4):
+            cols = slice(i * 256, (i + 1) * 256)
+            middle_ref[part, cols] = hidden_ref[part, cols].astype(F32) + through(
+                att_ref, part, OUT + (i // 2) * 512, quarters[i % 2]
+            )
+        middle = middle_ref[part, :]
+        ne_ref[part, :] = (middle * scale_of(middle) * small[1:2].astype(F32)).astype(BF16)
+        logits = dot(ne_ref[part, :], small, NT)
+        marks = mark_ref[part, :] > 0.0
+        peak = jnp.max(jnp.where(marks, logits, -1e30), axis=-1, keepdims=True)
+        lifted = jnp.where(marks, jnp.exp(jnp.where(marks, logits - peak, 0.0)), 0.0)
+        gates = lifted / jnp.sum(lifted, axis=-1, keepdims=True)
+        gate_ref[part, :] = gates
+
+        for e in range(3):
+            if e < 2:
+                ready(3 + e)
+            for lanes in quarters:
+                flat = slice(e * 512 + lanes.start, e * 512 + lanes.stop)
+                gl = through(ne_ref, part, EXPERT + e * 1024, lanes)
+                ul = through(ne_ref, part, EXPERT + e * 1024 + 512, lanes)
+                gl_ref[part, flat] = gl.astype(BF16)
+                ul_ref[part, flat] = ul.astype(BF16)
+                inner = gl * jax.nn.sigmoid(gl) * ul
+                gi_ref[part, flat] = (gates[:, 2 + e:3 + e] * inner).astype(BF16)
+
+        ready(5)
+        for i in range(4):
+            cols = slice(i * 256, (i + 1) * 256)
+            total = middle_ref[part, cols]
+            for e in range(3):
+                at = DOWN + e * 512 + (i // 2) * 256
+                for h in range(2):
+                    total = total + dot(
+                        gi_ref[part, e * 512 + h * 256:e * 512 + (h + 1) * 256],
+                        pool[h, at:at + 256, quarters[i % 2]], NN,
+                    )
+            output[part, cols] = total
+            for pack in range(part.start // 128, part.stop // 128):
+                at = pack * 128 - part.start
+                relay[pack, :, cols] = total[at:at + 128].astype(BF16)
+
     @pl.when(section == 0)
     def _():
         hidden_ref[...] = start_ref[...]
+        forward(slice(0, TOKENS), arrive)
+        for pack in range(2):
+            relays[pack].start()
+            relays[pack].wait_send()
 
     @pl.when(section == 1)
     def _():
-        for i in range(2):
-            relays[i].wait_recv()
-            hidden_ref[:, i * 512:(i + 1) * 512] = relayed[i]
-
-    pair.wait_recv()
-    small = jnp.concatenate([small_pair[0], small_pair[1]], axis=1)
-    x = hidden_ref[...].astype(F32)
-    normed_ref[...] = (x * scale_of(x) * small[0:1].astype(F32)).astype(BF16)
-
-    def through(a_ref, at, lanes):
-        return dot(a_ref[:, 0:512], pool[0, at:at + 512, lanes], NN) + dot(
-            a_ref[:, 512:1024], pool[1, at:at + 512, lanes], NN
-        )
-
-    quarters = (slice(0, 256), slice(256, 512))
-    for j, (target, at, turned) in enumerate(
-        ((q_ref, 0, True), (q_ref, 512, True), (k_ref, 0, True), (v_ref, 0, False))
-    ):
-        if j % 2 == 0:
-            arrive(j // 2)
-        for lanes in quarters:
-            u = through(normed_ref, j * 512, lanes)
-            if turned:
-                u = u * cos_ref[...] + swap_halves(u) * sin_ref[...]
-            target[:, at + lanes.start:at + lanes.stop] = u.astype(BF16)
-
-    for pack in range(2):
-        rows = slice(pack * 128, pack * 128 + 128)
-        bias = jnp.concatenate([bias_ref[pack], bias_ref[pack]], axis=0)
-        for pair_at in range(4):
-            keys = both_ways(k_ref[rows, pair_at * 128:(pair_at + 1) * 128])
-            values = both_ways(v_ref[rows, pair_at * 128:(pair_at + 1) * 128])
-            for half in range(2):
-                g = pair_at * 2 + half
-                queries = stack_heads(q_ref[rows, g * 128:(g + 1) * 128])
-                scores = dot(queries, keys[half], NT) * 0.125 + bias
-                exponent = jnp.exp(scores - jnp.max(scores, axis=-1, keepdims=True))
-                attention = (exponent / jnp.sum(exponent, axis=-1, keepdims=True)).astype(BF16)
-                p_ref[pack, g] = attention
-                att_ref[rows, g * 128:(g + 1) * 128] = join_heads(dot(attention, values[half], NN)).astype(BF16)
-
-    arrive(2)
-    for i in range(4):
-        cols = slice(i * 256, (i + 1) * 256)
-        middle_ref[:, cols] = hidden_ref[:, cols].astype(F32) + through(
-            att_ref, OUT + (i // 2) * 512, quarters[i % 2]
-        )
-    middle = middle_ref[...]
-    ne_ref[...] = (middle * scale_of(middle) * small[1:2].astype(F32)).astype(BF16)
-    logits = dot(ne_ref[...], small, NT)
-    peak = jnp.max(jnp.where(marks, logits, -1e30), axis=-1, keepdims=True)
-    lifted = jnp.where(marks, jnp.exp(jnp.where(marks, logits - peak, 0.0)), 0.0)
-    gates = lifted / jnp.sum(lifted, axis=-1, keepdims=True)
-
-    for e in range(3):
-        if e < 2:
-            arrive(3 + e)
-        for lanes in quarters:
-            flat = slice(e * 512 + lanes.start, e * 512 + lanes.stop)
-            gl = through(ne_ref, EXPERT + e * 1024, lanes)
-            ul = through(ne_ref, EXPERT + e * 1024 + 512, lanes)
-            gl_ref[:, flat] = gl.astype(BF16)
-            ul_ref[:, flat] = ul.astype(BF16)
-            inner = gl * jax.nn.sigmoid(gl) * ul
-            gi_ref[:, flat] = (gates[:, 2 + e:3 + e] * inner).astype(BF16)
-
-    arrive(5)
-    for i in range(4):
-        cols = slice(i * 256, (i + 1) * 256)
-        total = middle_ref[:, cols]
-        for e in range(3):
-            at = DOWN + e * 512 + (i // 2) * 256
-            for h in range(2):
-                total = total + dot(
-                    gi_ref[:, e * 512 + h * 256:e * 512 + (h + 1) * 256],
-                    pool[h, at:at + 256, quarters[i % 2]], NN,
-                )
-        output[:, cols] = total
-        relay[i // 2, :, quarters[i % 2]] = total.astype(BF16)
-        if i % 2 == 1:
-            @pl.when(section == 0)
-            def _():
-                relays[i // 2].start()
+        for i in range(len(PIECES)):
+            arrive(i)
+        for pack in range(2):
+            part = slice(pack * 128, pack * 128 + 128)
+            relays[pack].wait_recv()
+            hidden_ref[part, :] = relayed[pack]
+            forward(part, lambda i: None)
 
     output_copy = pltpu.make_async_copy(output, output_hbm, output_sem.at[0])
     output_copy.start()
 
-    @pl.when(section == 0)
-    def _():
-        for i in range(2):
-            relays[i].wait_send()
-        for i in range(2):
-            returns[i].wait_recv()
-            up_ref[:, i * 512:(i + 1) * 512] = returned[i]
-
-    @pl.when(section == 1)
-    def _():
-        up_ref[...] = loss_ref[...]
-
-    pulls = jnp.zeros((TOKENS, 16), F32)
-    for e in range(3):
-        gate = gates[:, 2 + e:3 + e]
-        for h in range(2):
-            flat = slice(e * 512 + h * 256, e * 512 + (h + 1) * 256)
-            at = DOWN + e * 512
-            u = dot(up_ref[:, 0:512], pool[h, at:at + 256, :], NT) + dot(
-                up_ref[:, 512:1024], pool[h, at + 256:at + 512, :], NT
-            )
-            gl = gl_ref[:, flat].astype(F32)
-            ul = ul_ref[:, flat].astype(F32)
-            sg = jax.nn.sigmoid(gl)
-            silu = gl * sg
-            pulls = pulls + jnp.where(lane == 2 + e, jnp.sum(u * silu * ul, axis=-1, keepdims=True), 0.0)
-            inner = gate * u
-            at = e * 1024 + h * 256
-            bgu_ref[:, at:at + 256] = (inner * ul * sg * (1.0 + gl * (1.0 - sg))).astype(BF16)
-            bgu_ref[:, at + 512:at + 768] = (inner * silu).astype(BF16)
-    back_logits = (gates * (pulls - jnp.sum(gates * pulls, axis=-1, keepdims=True))).astype(BF16)
-
-    for i in range(4):
-        cols = slice(i * 256, (i + 1) * 256)
-        h, inside = i // 2, (i % 2) * 256
-        total = dot(back_logits, small[:, cols], NN)
-        for j in range(6):
-            at = EXPERT + j * 512 + inside
-            total = total + dot(bgu_ref[:, j * 512:(j + 1) * 512], pool[h, at:at + 256, :], NT)
-        bne_ref[:, cols] = total
-    middle = middle_ref[...]
-    part, expert_gain = norm_back(middle, scale_of(middle), small[1:2].astype(F32), bne_ref[...])
-    bm_ref[...] = up_ref[...].astype(F32) + part
-    bb_ref[...] = bm_ref[...].astype(BF16)
-
-    for i in range(4):
-        h, inside = i // 2, (i % 2) * 256
-        total = dot(bb_ref[:, 0:512], pool[h, OUT + inside:OUT + inside + 256, :], NT)
-        total = total + dot(bb_ref[:, 512:1024], pool[h, OUT + 512 + inside:OUT + inside + 768, :], NT)
-        ba_ref[:, i * 256:(i + 1) * 256] = total.astype(BF16)
-
     cos, sin = cos_ref[0:128, 0:128], sin_ref[0:128, 0:128]
 
     def unturn(u):
         return (u * cos - swap_halves(u) * sin).astype(BF16)
 
     low = low_half((128, 128))
+    def backward(part):
+        gates = gate_ref[part, :]
+        lane = lax.broadcasted_iota(jnp.int32, (128, 16), 1)
+        pulls = jnp.zeros((128, 16), F32)
+        for e in range(3):
+            gate = gates[:, 2 + e:3 + e]
+            for h in range(2):
+                flat = slice(e * 512 + h * 256, e * 512 + (h + 1) * 256)
+                at = DOWN + e * 512
+                u = dot(up_ref[part, 0:512], pool[h, at:at + 256, :], NT) + dot(
+                    up_ref[part, 512:1024], pool[h, at + 256:at + 512, :], NT
+                )
+                gl = gl_ref[part, flat].astype(F32)
+                ul = ul_ref[part, flat].astype(F32)
+                sg = jax.nn.sigmoid(gl)
+                silu = gl * sg
+                pulls = pulls + jnp.where(lane == 2 + e, jnp.sum(u * silu * ul, axis=-1, keepdims=True), 0.0)
+                inner = gate * u
+                at = e * 1024 + h * 256
+                bgu_ref[part, at:at + 256] = (inner * ul * sg * (1.0 + gl * (1.0 - sg))).astype(BF16)
+                bgu_ref[part, at + 512:at + 768] = (inner * silu).astype(BF16)
+        back_logits = (gates * (pulls - jnp.sum(gates * pulls, axis=-1, keepdims=True))).astype(BF16)
+
+        for i in range(4):
+            cols = slice(i * 256, (i + 1) * 256)
+            h, inside = i // 2, (i % 2) * 256
+            total = dot(back_logits, small[:, cols], NN)
+            for j in range(6):
+                at = EXPERT + j * 512 + inside
+                total = total + dot(bgu_ref[part, j * 512:(j + 1) * 512], pool[h, at:at + 256, :], NT)
+            bne_ref[part, cols] = total
+        middle = middle_ref[part, :]
+        change, expert_gain = norm_back(middle, scale_of(middle), small[1:2].astype(F32), bne_ref[part, :])
+        bm_ref[part, :] = up_ref[part, :].astype(F32) + change
+        bb_ref[part, :] = bm_ref[part, :].astype(BF16)
+
+        for i in range(4):
+            h, inside = i // 2, (i % 2) * 256
+            total = dot(bb_ref[part, 0:512], pool[h, OUT + inside:OUT + inside + 256, :], NT)
+            total = total + dot(bb_ref[part, 512:1024], pool[h, OUT + 512 + inside:OUT + inside + 768, :], NT)
+            ba_ref[part, i * 256:(i + 1) * 256] = total.astype(BF16)
+
+        for pack in (part.start // 128,):
+            rows = slice(pack * 128, pack * 128 + 128)
+            for pair_at in range(4):
+                keys = both_ways(k_ref[rows, pair_at * 128:(pair_at + 1) * 128])
+                values = both_ways(v_ref[rows, pair_at * 128:(pair_at + 1) * 128])
+                back_k, back_v = [], []
+                for half in range(2):
+                    g = pair_at * 2 + half
+                    cols = slice(g * 128, (g + 1) * 128)
+                    queries = stack_heads(q_ref[rows, cols])
+                    back_out = stack_heads(ba_ref[rows, cols])
+                    attention = p_ref[pack, g]
+                    wide = attention.astype(F32)
+                    pull = dot(back_out, values[half], NT)
+                    bv = dot(attention, back_out, TN)
+                    back_v.append(bv + pltpu.roll(bv, 64, 1))
+                    spread = wide * pull
+                    back_scores = (
+                        (spread - wide * jnp.sum(spread, axis=-1, keepdims=True)) * 0.125
+                    ).astype(BF16)
+                    bqkv_ref[rows, cols] = unturn(join_heads(dot(back_scores, keys[half], NN)))
+                    bk = dot(back_scores, queries, TN)
+                    back_k.append(bk + pltpu.roll(bk, 64, 1))
+                at = 1024 + pair_at * 128
+                bqkv_ref[rows, at:at + 128] = unturn(jnp.where(low, back_k[0], back_k[1]))
+                bqkv_ref[rows, at + 512:at + 640] = jnp.where(low, back_v[0], back_v[1]).astype(BF16)
+
+        for i in range(4):
+            h, inside = i // 2, (i % 2) * 256
+            total = jnp.zeros((128, 256), F32)
+            for j in range(4):
+                at = j * 512 + inside
+                total = total + dot(bqkv_ref[part, j * 512:(j + 1) * 512], pool[h, at:at + 256, :], NT)
+            bne_ref[part, i * 256:(i + 1) * 256] = total
+        x = hidden_ref[part, :].astype(F32)
+        change, mixer_gain = norm_back(x, scale_of(x), small[0:1].astype(F32), bne_ref[part, :])
+        gradient[part, :] = bm_ref[part, :] + change
+        relay[part.start // 128] = gradient[part, :].astype(BF16)
+        router = dot(back_logits, ne_ref[part, :], TN)
+        row = lax.broadcasted_iota(jnp.int32, router.shape, 0)
+        return jnp.where(row == 0, mixer_gain, jnp.where(row == 1, expert_gain, router))
+
+    mixed = jnp.zeros((16, WIDTH), F32)
     for pack in range(2):
-        rows = slice(pack * 128, pack * 128 + 128)
-        for pair_at in range(4):
-            keys = both_ways(k_ref[rows, pair_at * 128:(pair_at + 1) * 128])
-            values = both_ways(v_ref[rows, pair_at * 128:(pair_at + 1) * 128])
-            back_k, back_v = [], []
-            for half in range(2):
-                g = pair_at * 2 + half
-                cols = slice(g * 128, (g + 1) * 128)
-                queries = stack_heads(q_ref[rows, cols])
-                back_out = stack_heads(ba_ref[rows, cols])
-                attention = p_ref[pack, g]
-                wide = attention.astype(F32)
-                pull = dot(back_out, values[half], NT)
-                bv = dot(attention, back_out, TN)
-                back_v.append(bv + pltpu.roll(bv, 64, 1))
-                spread = wide * pull
-                back_scores = (
-                    (spread - wide * jnp.sum(spread, axis=-1, keepdims=True)) * 0.125
-                ).astype(BF16)
-                bqkv_ref[rows, cols] = unturn(join_heads(dot(back_scores, keys[half], NN)))
-                bk = dot(back_scores, queries, TN)
-                back_k.append(bk + pltpu.roll(bk, 64, 1))
-            at = 1024 + pair_at * 128
-            bqkv_ref[rows, at:at + 128] = unturn(jnp.where(low, back_k[0], back_k[1]))
-            bqkv_ref[rows, at + 512:at + 640] = jnp.where(low, back_v[0], back_v[1]).astype(BF16)
-
-    for i in range(4):
-        h, inside = i // 2, (i % 2) * 256
-        total = jnp.zeros((TOKENS, 256), F32)
-        for j in range(4):
-            at = j * 512 + inside
-            total = total + dot(bqkv_ref[:, j * 512:(j + 1) * 512], pool[h, at:at + 256, :], NT)
-        bne_ref[:, i * 256:(i + 1) * 256] = total
-    x = hidden_ref[...].astype(F32)
-    part, mixer_gain = norm_back(x, scale_of(x), small[0:1].astype(F32), bne_ref[...])
-    gradient[...] = bm_ref[...] + part
-    for i in range(2):
-        relay[i] = gradient[:, i * 512:(i + 1) * 512].astype(BF16)
-
-    @pl.when(section == 1)
-    def _():
-        for i in range(2):
-            returns[i].start()
+        part = slice(pack * 128, pack * 128 + 128)
+
+        @pl.when(section == 0)
+        def _():
+            returns[pack].wait_recv()
+            up_ref[part, :] = returned[pack]
+
+        @pl.when(section == 1)
+        def _():
+            up_ref[part, :] = loss_ref[part, :]
+
+        mixed = mixed + backward(part)
+
+        @pl.when(section == 1)
+        def _():
+            returns[pack].start()
 
     gradient_copy = pltpu.make_async_copy(gradient, gradient_hbm, output_sem.at[1])
     gradient_copy.start()
-    router = dot(back_logits, ne_ref[...], TN)
-    row = lax.broadcasted_iota(jnp.int32, router.shape, 0)
-    mixed = jnp.where(row == 0, mixer_gain, jnp.where(row == 1, expert_gain, router))
     small_mine[0] = mixed[:, 0:512]
     small_mine[1] = mixed[:, 512:1024]
 
@@ -439,9 +458,15 @@
                 for i in range(2):
                     tile(gi_ref, e * 512 + half * 256, 256, up_ref, i * 512, DOWN + e * 512 + i * 256)
 
-    for copy in sends:
+    for copy in given + [pair]:
         copy.wait_send()
     sends.clear()
+
+    @pl.when(section == 1)
+    def _():
+        for i in range(2):
+            returns[i].wait_send()
+
     lent = pool.at[1 - core]
     size = [PART >> s for s in range(DIMS + 1)]
     bit = [[bits[(p + s) % DIMS] for s in range(DIMS)] for p in range(PARTS)]
@@ -566,11 +591,6 @@
                 shared[p][(s - 2, 0)] = share(p, s - 2, held[p][s], 0)
             store(got, size[s + 1])
 
-    @pl.when(section == 1)
-    def _():
-        for i in range(2):
-            returns[i].wait_send()
-
     for copy in sends:
         copy.wait_send()
     for copy in stores:
@@ -586,7 +606,8 @@
 def both_layers(operands, weights):
     dma = pltpu.SemaphoreType.DMA
     wide, narrow = pltpu.VMEM((TOKENS, WIDTH), F32), pltpu.VMEM((TOKENS, WIDTH), BF16)
-    halves = pltpu.VMEM((2, TOKENS, 512), BF16)
+    halves = pltpu.VMEM((2, 128, WIDTH), BF16)
+    column = pltpu.VMEM((TOKENS, 16), F32)
     buffer = pltpu.VMEM((ROWS, COLS), BF16)
     inner = pltpu.VMEM((TOKENS, 1536), BF16)
     return pl.pallas_call(
@@ -603,7 +624,7 @@
             pltpu.VMEM((2, ROWS, COLS), BF16), buffer, buffer, buffer,
             pltpu.VMEM((2, 16, COLS), BF16), pltpu.VMEM((2, 16, COLS), F32),
             pltpu.VMEM((DIMS, 16, COLS), F32), pltpu.VMEM((DIMS + 1, 16, COLS), F32),
-            halves, halves, halves, wide, pltpu.VMEM((2, 128, 128), F32),
+            halves, halves, halves, wide, pltpu.VMEM((2, 128, 128), F32), column, column,
             narrow, narrow, narrow, pltpu.VMEM((TOKENS, 512), BF16), pltpu.VMEM((TOKENS, 512), BF16),
             pltpu.VMEM((2, 8, 256, 128), BF16), narrow, wide, narrow, inner, inner, inner,
             narrow, pltpu.VMEM((TOKENS, 3072), BF16), narrow, pltpu.VMEM((TOKENS, 2048), BF16),
@@ -727,7 +748,7 @@
         gradient.reshape(1, 2, 1, 128, WIDTH),
         owned[0],
     ) + tuple(item[None] for item in owned[1:5]) + (owned[5],) + (
-        jnp.transpose(owned[6][:, 0])[None],
+        jnp.transpose(owned[6], (1, 2, 0)),
     ) + tuple(item[None] for item in owned[7:])
 
 

time: 179 us -> 169 us (0.944)
  Pallas kernels: 177 us -> 168 us
    pallas_call x1, Pallas kernels: 166 us -> 158 us  [both_layers(): pl.pallas_call(layer_kernel, out_shape=(jax.ShapeDtypeStruct((TOKENS, WID...]
where the time goes in v1:
time: 169 us
  Pallas kernels  168 us (99%)
    pallas_call x1, Pallas kernels, both_layers(): pl.pallas_call(layer_kernel, out_shape=(jax.ShapeDtypeStruct((TOKENS, WID...  158 us
    pallas_call x1, Pallas kernels, unpack(): pl.pallas_call(unpack_kernel, out_shape=tuple((jax.ShapeDtypeStruct(shape...  10.8 us

profile of v1, /device:TPU:0, one launch (start us, length us, event | category | flops | bytes accessed | tf_op | source)
XLA Modules:
  0.0 169.2 jit_solution(1386400699301427821)
XLA Ops:
  0.6 157.5 %shard_map.247 = (f32[256,1024]{1,0:T(8,128)}, f32[256,1024]{1,0:T(8,128)}, bf16[7680,512]{1,0:T(8,128)(2,1)}, f32[16,512]{1,0:T(8,128)}) custom-call(bf16[256,1024]{1,0:T(8,128)(2,1)} %bitcast.35, bf16[256,1024]{1,0:T(8,128)(2,1)} %bitcast.36, s32[2,128]{1,0:T(2,128)} %bitcast.41, s32[2,2,128]{2,1,0:T(2,128)} %bitcast.40, bf16[1,512]{1,0:T(2,128)(2,1)} %mixer_ref.1, ...), custom_call_target="tpu_custom_call" | custom-call | tf_op jit(solution)/shard_map/pallas_call | solution.py:613
  158.2 10.8 %shard_map.248 = (f32[1,512]{1,0:T(1,128)}, f32[512,1024]{1,0:T(8,128)}, f32[512,512]{1,0:T(8,128)}, f32[512,512]{1,0:T(8,128)}, f32[512,1024]{1,0:T(8,128)}, /*...) custom-call(bf16[7680,512]{1,0:T(8,128)(2,1)} %get-tuple-element.28., ...), custom_call_target="tpu_custom_call" | custom-call | tf_op jit(solution)/shard_map/pallas_call | solution.py:710
